TPU v7x, 32 devices: a whole 2x2x4 slice. The times are simulated.
32 devices in a mesh: group: 2 (over x), frame: 16 (over z, y, core).
Axes of the slice: x: 2, y: 2, z: 4, core: 2. Of those that a mesh axis runs over, the one named last changes fastest.
Arguments:
- queries: bfloat16 [10240, 5120], P(('group', 'frame')), parts along dimension 0, may hold values from -33 to 33
- keys: bfloat16 [10240, 5120], P(('group', 'frame')), parts along dimension 0, may hold values from -33 to 33
- values: bfloat16 [10240, 5120], P(('group', 'frame')), parts along dimension 0, may hold values from -6 to 6
- labels: int32 [80], P('group'), parts along dimension 0, may hold values from 0 to 1, as said below
- band: int32 [80], P('group'), parts along dimension 0, may hold values from 2 to 4
Outputs:
- attended: bfloat16 [10240, 5120], P(('group', 'frame')), parts along dimension 0
There are 2 independent parts, one for each index of `group`. A program takes and returns all parts, laid end to end along the dimension named above; each array names one. Nothing has to cross between parts.
Inputs may be any that keep to these rules, and one draw needn't show every extreme that they name: `labels`: exactly 10 of the 40 heads carry 1, the others 0.
All inputs are finite; a program needn't handle non-finite values.
Results may differ from a plain program's by a relative error of at most 0.0049.
Values may be sent and summed in bfloat16 or wider, within the bound.
A program may use at most 128 MiB of HBM per device.

v0:
```python
import math
import jax
import jax.numpy as jnp
from jax import lax
from jax.sharding import PartitionSpec as P

TEMP_HEADS = 10


def from_partner(block, axis, bit):
    count = lax.axis_size(axis)
    route = []
    for low in range(count):
        high = low | 1 << bit
        if high != low and high < count:
            route += [(low, high), (high, low)]
    return lax.ppermute(block, axis, route)


def softmax_rounded(scores):
    peak = jnp.max(scores, axis=-1, keepdims=True)
    weights = jnp.exp(scores - peak)
    return (weights / jnp.sum(weights, axis=-1, keepdims=True)).astype(jnp.bfloat16)


def block_heads(count):
    for candidate in (6, 5, 4, 3, 2):
        if count % candidate == 0:
            return candidate
    return 1


def attend_spatial(query_part, key_all, value_all):
    head_total = query_part.shape[1]
    step_heads = block_heads(head_total)
    scale = 1.0 / math.sqrt(query_part.shape[2])

    def one_block(block_number, result):
        start = block_number * step_heads
        query_block = lax.dynamic_slice_in_dim(query_part, start, step_heads, 1)
        key_block = lax.dynamic_slice_in_dim(key_all, start, step_heads, 1)
        value_block = lax.dynamic_slice_in_dim(value_all, start, step_heads, 1)
        scores = (
            jnp.einsum("rhd,khd->hrk", query_block, key_block, preferred_element_type=jnp.float32)
            * scale
        )
        weights = softmax_rounded(scores)
        output_block = jnp.einsum(
            "hrk,khd->rhd", weights, value_block, preferred_element_type=jnp.float32
        ).astype(jnp.bfloat16)
        return lax.dynamic_update_slice_in_dim(result, output_block, start, 1)

    initial = jnp.zeros(query_part.shape, jnp.bfloat16)
    return lax.fori_loop(0, head_total // step_heads, one_block, initial)


def attend_columns(query_part, key_part, value_part, head_band):
    query_cols, key_cols, value_cols = (
        lax.all_to_all(query_part[None], "frame", split_axis=1, concat_axis=0, tiled=True),
        lax.all_to_all(key_part[None], "frame", split_axis=1, concat_axis=0, tiled=True),
        lax.all_to_all(value_part[None], "frame", split_axis=1, concat_axis=0, tiled=True),
    )
    sources, pixels, head_part, head_size = query_cols.shape
    frames = sources // 2
    scale = 1.0 / math.sqrt(head_size)
    grid_shape = (frames, 2, pixels, head_part, head_size)
    scores = (
        jnp.einsum(
            "fapnd,gapnd->apnfg",
            query_cols.reshape(grid_shape),
            key_cols.reshape(grid_shape),
            preferred_element_type=jnp.float32,
        )
        * scale
    )
    frame_ids = jnp.arange(frames, dtype=jnp.int32)
    distance = jnp.abs(frame_ids[:, None] - frame_ids[None, :])
    keep = distance[None, :, :] <= head_band[:, None, None]
    scores = jnp.where(keep, scores, jnp.float32(-1e30))
    weights = softmax_rounded(scores)
    output = jnp.einsum(
        "apnfg,gapnd->fapnd",
        weights,
        value_cols.reshape(grid_shape),
        preferred_element_type=jnp.float32,
    ).astype(jnp.bfloat16)
    output = output.reshape(sources, pixels, head_part, head_size)
    returned = lax.all_to_all(output, "frame", split_axis=0, concat_axis=1, tiled=True)
    return returned[0]


def shards(queries, keys, values, labels, band):
    row_count = queries.shape[0]
    head_count = labels.shape[0]
    head_size = queries.shape[1] // head_count
    query_heads = queries.reshape(row_count, head_count, head_size)
    key_heads = keys.reshape(row_count, head_count, head_size)
    value_heads = values.reshape(row_count, head_count, head_size)
    spatial_count = head_count - TEMP_HEADS
    ordering = jnp.argsort(labels, stable=True)
    spatial_index = ordering[:spatial_count]
    temporal_index = ordering[spatial_count:]
    inverse = jnp.argsort(ordering, stable=True)
    query_spatial = jnp.take(query_heads, spatial_index, axis=1)
    key_spatial = jnp.take(key_heads, spatial_index, axis=1)
    value_spatial = jnp.take(value_heads, spatial_index, axis=1)
    temporal_band = jnp.take(band, temporal_index)
    temporal = attend_columns(
        jnp.take(query_heads, temporal_index, axis=1),
        jnp.take(key_heads, temporal_index, axis=1),
        jnp.take(value_heads, temporal_index, axis=1),
        temporal_band,
    )
    parity = lax.axis_index("frame") % 2
    half = spatial_count // 2
    mine_start = parity * half
    other_start = (1 - parity) * half
    query_mine = lax.dynamic_slice_in_dim(query_spatial, mine_start, half, 1)
    key_mine = lax.dynamic_slice_in_dim(key_spatial, mine_start, half, 1)
    value_mine = lax.dynamic_slice_in_dim(value_spatial, mine_start, half, 1)
    query_other = lax.dynamic_slice_in_dim(query_spatial, other_start, half, 1)
    key_other = lax.dynamic_slice_in_dim(key_spatial, other_start, half, 1)
    value_other = lax.dynamic_slice_in_dim(value_spatial, other_start, half, 1)
    query_got, key_got, value_got = from_partner((query_other, key_other, value_other), "frame", 0)

    def whole_frame(own, got):
        return jnp.where(
            parity == 0, jnp.concatenate([own, got], axis=0), jnp.concatenate([got, own], axis=0)
        )

    frame_out = attend_spatial(
        whole_frame(query_mine, query_got),
        whole_frame(key_mine, key_got),
        whole_frame(value_mine, value_got),
    )
    own_rows = lax.dynamic_slice_in_dim(frame_out, parity * row_count, row_count, 0)
    other_rows = lax.dynamic_slice_in_dim(frame_out, (1 - parity) * row_count, row_count, 0)
    returned = from_partner(other_rows, "frame", 0)
    spatial = jnp.where(
        parity == 0,
        jnp.concatenate([own_rows, returned], axis=1),
        jnp.concatenate([returned, own_rows], axis=1),
    )
    combined = jnp.take(jnp.concatenate([spatial, temporal], axis=1), inverse, axis=1)
    return combined.reshape(row_count, head_count * head_size)


def solution(mesh):
    placed = (
        P(("group", "frame"), None),
        P(("group", "frame"), None),
        P(("group", "frame"), None),
        P("group"),
        P("group"),
    )
    return jax.shard_map(
        shards, mesh=mesh, in_specs=placed, out_specs=P(("group", "frame"), None), check_vma=False
    )
```

profile of v0, /device:TPU:9, one launch (start us, length us, event | category | flops | bytes accessed | tf_op | source)
XLA Modules:
  0.0 212.5 jit_solution(6797831736654225508)
XLA Ops:
  0.0 1.9 copy-done
  1.9 2.6 %copy_bitcast_fusion.1 = bf16[320,40,128]{2,0,1:T(8,128)(2,1)} fusion(bf16[320,5120]{1,0:T(8,128)(2,1)S(1)} %copy-done), kind=kLoop, calls=%fused_computation.30 | loop fusion | bytes 6553600 | tf_op jit(solution)/shard_map/reshape | solution.py:96
  4.6 2.0 sort.31
  6.7 4.7 %copy_bitcast_fusion = bf16[320,40,128]{2,0,1:T(8,128)(2,1)} fusion(bf16[320,5120]{1,0:T(8,128)(2,1)} %param.12), kind=kLoop, calls=%fused_computation.29 | loop fusion | bytes 6553600 | tf_op jit(solution)/shard_map/reshape | solution.py:97
  11.3 1.6 gather_fusion.6
  13.0 3.5 %gather_fusion.7 = bf16[10,320,128]{2,1,0:T(8,128)(2,1)} fusion(bf16[320,40,128]{2,0,1:T(8,128)(2,1)} %copy_bitcast_fusion, s32[1024]{0:T(1024)S(1)} %pad_clamp_fusion.1), kind=kCustom, calls=%fused_computation.5.clone | custom fusion | bytes 1638440 | tf_op jit(solution)/shard_map/jit(_take)/gather | solution.py:110
  16.5 4.5 %copy_bitcast_fusion.2 = bf16[320,40,128]{2,0,1:T(8,128)(2,1)} fusion(bf16[320,5120]{1,0:T(8,128)(2,1)} %param.13), kind=kLoop, calls=%fused_computation.31 | loop fusion | bytes 6553600 | tf_op jit(solution)/shard_map/reshape | solution.py:98
  21.0 3.5 %gather_fusion.5 = bf16[10,320,128]{2,1,0:T(8,128)(2,1)} fusion(bf16[320,40,128]{2,0,1:T(8,128)(2,1)} %copy_bitcast_fusion.2, s32[1024]{0:T(1024)S(1)} %pad_clamp_fusion.1), kind=kCustom, calls=%fused_computation.1.clone | custom fusion | bytes 1638440 | tf_op jit(solution)/shard_map/jit(_take)/gather | solution.py:111
  24.6 3.1 %select_bitcast_fusion.4 = (bf16[1,320,10,128]{3,1,2,0:T(8,128)(2,1)}, bf16[1,320,10,128]{3,1,2,0:T(8,128)(2,1)S(1)}, bf16[1,320,10,128]{3,1,2,0:T(8,128)(2,1)}) fusion(bf16[10,320,128]{2,1,0:T(8,128)(2,1)} %gather_fusion.6, pred[10]{0:T(512)(128)(4,1)S(1)} %get-tuple-element.148, bf16[10,320,128]{2,1,0:T(8,128)(2,1)} %gather_fusion.7, ...), kind=kLoop, calls=%fused_computation.50 | loop fusion | flops 1228800 | bytes 4915210 | tf_op jit(solution)/shard_map/broadcast_in_dim | solution.py:59
  27.7 1.7 copy.97
  29.4 6.6 %all-to-all-start.2 = ((bf16[1,320,10,128]{3,2,0,1:T(8,128)(2,1)}), bf16[1,320,10,128]{3,2,0,1:T(8,128)(2,1)}, u32[]{:S(2)}, u32[]{:S(2)}) async-start(bf16[1,320,10,128]{3,2,0,1:T(8,128)(2,1)} %copy.97), calls=%async_computation.2 | async-start | bytes 2621440 | tf_op jit(solution)/shard_map/all_to_all | solution.py:60
  36.1 4.3 %gather_fusion.4 = bf16[30,320,128]{2,1,0:T(8,128)(2,1)} fusion(bf16[320,40,128]{2,0,1:T(8,128)(2,1)} %copy_bitcast_fusion, s32[1024]{0:T(1024)S(1)} %pad_clamp_fusion.2), kind=kCustom, calls=%fused_computation.3.clone | custom fusion | bytes 4915320 | tf_op jit(solution)/shard_map/jit(_take)/gather | solution.py:105
  40.4 2.3 %gather_fusion.3 = bf16[30,320,128]{2,1,0:T(8,128)(2,1)} fusion(bf16[320,40,128]{2,0,1:T(8,128)(2,1)S(1)} %copy-done.4, s32[1024]{0:T(1024)S(1)} %pad_clamp_fusion.2), kind=kCustom, calls=%fused_computation.2.clone | custom fusion | bytes 4915320 | tf_op jit(solution)/shard_map/jit(_take)/gather | solution.py:104
  42.7 4.4 %gather_fusion.2 = bf16[30,320,128]{2,1,0:T(8,128)(2,1)} fusion(bf16[320,40,128]{2,0,1:T(8,128)(2,1)} %copy_bitcast_fusion.2, s32[1024]{0:T(1024)S(1)} %pad_clamp_fusion.2), kind=kCustom, calls=%fused_computation.clone | custom fusion | bytes 4915320 | tf_op jit(solution)/shard_map/jit(_take)/gather | solution.py:106
  47.1 4.6 %select_bitcast_fusion = (bf16[320,30,128]{2,0,1:T(8,128)(2,1)}, bf16[320,30,128]{2,0,1:T(8,128)(2,1)S(1)}, bf16[320,30,128]{2,0,1:T(8,128)(2,1)S(1)}) fusion(bf16[30,320,128]{2,1,0:T(8,128)(2,1)S(1)} %copy-done.5, pred[30]{0:T(512)(128)(4,1)S(1)} %get-tuple-element.146, bf16[30,320,128]{2,1,0:T(8,128)(2,1)} %gather_fusion.3, ...), kind=kLoop, calls=%fused_computation.37 | loop fusion | flops 3686400 | bytes 14745630 | tf_op jit(solution)/shard_map/jit(_take)/select_n | solution.py:105
  53.6 1.6 constant_dynamic-slice_fusion.5
  55.4 1.7 copy.94
  57.1 9.3 %all-to-all-done.2 = bf16[1,320,10,128]{3,2,0,1:T(8,128)(2,1)} async-done(((bf16[1,320,10,128]{3,2,0,1:T(8,128)(2,1)}), bf16[1,320,10,128]{3,2,0,1:T(8,128)(2,1)}, u32[]{:S(2)}, u32[]{:S(2)}) %all-to-all-start.2) | async-done | bytes 819232 | tf_op jit(solution)/shard_map/all_to_all | solution.py:60
  66.3 5.2 %all-to-all-start.1 = ((bf16[1,320,10,128]{3,2,0,1:T(8,128)(2,1)}), bf16[1,320,10,128]{3,2,0,1:T(8,128)(2,1)}, u32[]{:S(2)}, u32[]{:S(2)}) async-start(bf16[1,320,10,128]{3,2,0,1:T(8,128)(2,1)} %copy.94), calls=%async_computation.1 | async-start | bytes 2621440 | tf_op jit(solution)/shard_map/all_to_all | solution.py:59
  71.6 1.6 constant_dynamic-slice_fusion.3
  73.6 2.8 %copy.91 = bf16[1,320,10,128]{3,2,0,1:T(8,128)(2,1)} copy(bf16[1,320,10,128]{3,1,2,0:T(8,128)(2,1)} %get-tuple-element.163) | data formatting | bytes 1638400 | tf_op jit(solution)/shard_map/broadcast_in_dim | solution.py:61
  77.2 4.0 %maximum_select_fusion = bf16[640,15,128]{2,0,1:T(8,128)(2,1)} fusion(bf16[320,15,128]{2,0,1:T(8,128)(2,1)} %collective-permute-done, bf16[320,15,128]{2,0,1:T(8,128)(2,1)S(1)} %copy-done.8, pred[]{:T(512)S(6)} %eq.4), kind=kLoop, calls=%fused_computation.33 | loop fusion | flops 11059200 | bytes 4915201 | tf_op jit(solution)/shard_map/jit(_where)/select_n | solution.py:127
  81.2 4.0 %maximum_select_fusion.1 = bf16[640,15,128]{2,0,1:T(8,128)(2,1)} fusion(bf16[320,15,128]{2,0,1:T(8,128)(2,1)} %collective-permute-done.1, bf16[320,15,128]{2,0,1:T(8,128)(2,1)S(1)} %copy-done.9, pred[]{:T(512)S(6)} %eq.4), kind=kLoop, calls=%fused_computation.34 | loop fusion | flops 11059200 | bytes 4915201 | tf_op jit(solution)/shard_map/jit(_where)/select_n | solution.py:127
  85.2 3.8 %maximum_select_fusion.2 = bf16[640,15,128]{2,0,1:T(8,128)(2,1)} fusion(bf16[320,15,128]{2,0,1:T(8,128)(2,1)} %collective-permute-done.2, bf16[320,15,128]{2,0,1:T(8,128)(2,1)S(1)} %copy-done.10, pred[]{:T(512)S(6)} %eq.4), kind=kLoop, calls=%fused_computation.35 | loop fusion | flops 11059200 | bytes 4915201 | tf_op jit(solution)/shard_map/jit(_where)/select_n | solution.py:127
  89.0 12.9 %all-to-all-done.1 = bf16[1,320,10,128]{3,2,0,1:T(8,128)(2,1)} async-done(((bf16[1,320,10,128]{3,2,0,1:T(8,128)(2,1)}), bf16[1,320,10,128]{3,2,0,1:T(8,128)(2,1)}, u32[]{:S(2)}, u32[]{:S(2)}) %all-to-all-start.1) | async-done | bytes 819232 | tf_op jit(solution)/shard_map/all_to_all | solution.py:59
  101.9 5.3 %all-to-all-start = ((bf16[1,320,10,128]{3,2,0,1:T(8,128)(2,1)}), bf16[1,320,10,128]{3,2,0,1:T(8,128)(2,1)S(1)}, u32[]{:S(2)}, u32[]{:S(2)}) async-start(bf16[1,320,10,128]{3,2,0,1:T(8,128)(2,1)} %copy.91), calls=%async_computation | async-start | bytes 2621440 | tf_op jit(solution)/shard_map/all_to_all | solution.py:61
  107.1 1.9 broadcast_in_dim.73.clone
  109.0 50.4 %while.13 = (s32[]{:T(128)}, bf16[640,15,128]{2,0,1:T(8,128)(2,1)}, bf16[640,15,128]{2,0,1:T(8,128)(2,1)}, bf16[640,15,128]{2,0,1:T(8,128)(2,1)}, bf16[640,15,12...) while((s32[]{:T(128)}, bf16[640,15,128]{2,0,1:T(8,128)(2,1)}, ...), condition=%wide.region_5.7_spmd, body=%wide.region_2.6_spmd.sunk | while | flops 1067422080 | bytes 72116400 | solution.py:54
  109.0 2.6 %fusion.48 = f32[5,640,640]{1,2,0:T(8,128)S(1)} fusion(bf16[640,15,128]{2,0,1:T(8,128)(2,1)} %get-tuple-element.219, s32[]{:T(128)S(6)} %select_n.164, bf16[640,15,128]{2,0,1:T(8,128)(2,1)} %get-tuple-element.218), kind=kOutput, calls=%fused_computation.17.clone.1 | convolution fusion | flops 524288000 | bytes 9831424 | tf_op jit(solution)/shard_map/while/body/eval_jaxpr/rhd,khd->hrk/dot_general | solution.py:44
  111.7 2.1 fusion.49
  114.8 8.7 %fusion.50 = bf16[640,5,128]{0,2,1:T(8,128)(2,1)S(1)} fusion(f32[5,640]{1,0:T(8,128)S(1)} %fusion.49, bf16[640,15,128]{2,0,1:T(8,128)(2,1)} %get-tuple-element.217, s32[]{:T(128)S(6)} %select_n.164, f32[5,640,640]{1,2,0:T(8,128)} %copy-done.3), kind=kOutput, calls=%fused_computation.16.clone.1 | convolution fusion | flops 534941440 | bytes 18035204 | tf_op jit(solution)/shard_map/while/body/eval_jaxpr/hrk,khd->rhd/dot_general | solution.py:48
  125.8 2.6 %fusion.48 = f32[5,640,640]{1,2,0:T(8,128)S(1)} fusion(bf16[640,15,128]{2,0,1:T(8,128)(2,1)} %get-tuple-element.219, s32[]{:T(128)S(6)} %select_n.164, bf16[640,15,128]{2,0,1:T(8,128)(2,1)} %get-tuple-element.218), kind=kOutput, calls=%fused_computation.17.clone.1 | convolution fusion | flops 524288000 | bytes 9831424 | tf_op jit(solution)/shard_map/while/body/eval_jaxpr/rhd,khd->hrk/dot_general | solution.py:44
  128.5 2.1 fusion.49
  131.6 8.7 %fusion.50 = bf16[640,5,128]{0,2,1:T(8,128)(2,1)S(1)} fusion(f32[5,640]{1,0:T(8,128)S(1)} %fusion.49, bf16[640,15,128]{2,0,1:T(8,128)(2,1)} %get-tuple-element.217, s32[]{:T(128)S(6)} %select_n.164, f32[5,640,640]{1,2,0:T(8,128)} %copy-done.3), kind=kOutput, calls=%fused_computation.16.clone.1 | convolution fusion | flops 534941440 | bytes 18035204 | tf_op jit(solution)/shard_map/while/body/eval_jaxpr/hrk,khd->rhd/dot_general | solution.py:48
  142.6 2.6 %fusion.48 = f32[5,640,640]{1,2,0:T(8,128)S(1)} fusion(bf16[640,15,128]{2,0,1:T(8,128)(2,1)} %get-tuple-element.219, s32[]{:T(128)S(6)} %select_n.164, bf16[640,15,128]{2,0,1:T(8,128)(2,1)} %get-tuple-element.218), kind=kOutput, calls=%fused_computation.17.clone.1 | convolution fusion | flops 524288000 | bytes 9831424 | tf_op jit(solution)/shard_map/while/body/eval_jaxpr/rhd,khd->hrk/dot_general | solution.py:44
  145.2 2.1 fusion.49
  148.4 8.7 %fusion.50 = bf16[640,5,128]{0,2,1:T(8,128)(2,1)S(1)} fusion(f32[5,640]{1,0:T(8,128)S(1)} %fusion.49, bf16[640,15,128]{2,0,1:T(8,128)(2,1)} %get-tuple-element.217, s32[]{:T(128)S(6)} %select_n.164, f32[5,640,640]{1,2,0:T(8,128)} %copy-done.3), kind=kOutput, calls=%fused_computation.16.clone.1 | convolution fusion | flops 534941440 | bytes 18035204 | tf_op jit(solution)/shard_map/while/body/eval_jaxpr/hrk,khd->rhd/dot_general | solution.py:48
  159.4 4.2 %exponential_reduce_fusion = (f32[2,20,10,8]{3,2,1,0:T(8,128)}, f32[2,20,10,8,8]{3,4,2,1,0:T(8,128)S(1)}) fusion(bf16[8,2,20,10,128]{4,3,2,1,0:T(8,128)(2,1)} %bitcast.13, bf16[8,2,20,10,128]{4,3,2,1,0:T(8,128)(2,1)} %bitcast.10, pred[10,8,8]{1,2,0:T(8,128)(4,1)S(1)} %broadcast_compare_fusion), kind=kOutput, calls=%fused_computation.43 | convolution fusion | flops 6656007 | bytes 1754240 | tf_op jit(solution)/shard_map/sub | solution.py:22
  163.6 1.8 fusion.24
  168.0 6.0 %all-to-all-start.3 = ((bf16[16,20,10,128]{3,1,2,0:T(8,128)(2,1)}), bf16[16,20,10,128]{3,1,2,0:T(8,128)(2,1)}, u32[]{:S(2)}, u32[]{:S(2)}) async-start(bf16[16,20,10,128]{3,1,2,0:T(8,128)(2,1)} %copy.104), calls=%async_computation.3 | async-start | bytes 1966080 | tf_op jit(solution)/shard_map/all_to_all | solution.py:88
  174.1 1.6 constant_dynamic-slice_fusion.1
  176.1 2.1 sort.32
  179.9 2.7 %maximum_select_fusion.3 = bf16[320,30,128]{2,0,1:T(8,128)(2,1)S(1)} fusion(bf16[320,15,128]{2,0,1:T(8,128)(2,1)} %copy-done.12, bf16[320,15,128]{2,0,1:T(8,128)(2,1)} %get-tuple-element.150, pred[]{:T(512)S(6)} %eq.4), kind=kLoop, calls=%fused_computation.36 | loop fusion | flops 3686400 | bytes 4915201 | tf_op jit(solution)/shard_map/jit(_where)/select_n | solution.py:139
  182.6 15.1 %all-to-all-done.3 = bf16[16,20,10,128]{3,1,2,0:T(8,128)(2,1)} async-done(((bf16[16,20,10,128]{3,1,2,0:T(8,128)(2,1)}), bf16[16,20,10,128]{3,1,2,0:T(8,128)(2,1)}, u32[]{:S(2)}, u32[]{:S(2)}) %all-to-all-start.3) | async-done | bytes 819232 | tf_op jit(solution)/shard_map/all_to_all | solution.py:88
  197.7 2.4 %copy.105 = bf16[16,20,10,128]{3,1,0,2:T(8,128)(2,1)} copy(bf16[16,20,10,128]{3,1,2,0:T(8,128)(2,1)} %all-to-all-done.3) | data formatting | bytes 1638400 | tf_op jit(solution)/shard_map/all_to_all | solution.py:88
  201.3 2.0 pad_maximum_fusion
  203.3 4.9 %gather_fusion.1 = bf16[40,320,128]{2,1,0:T(8,128)(2,1)} fusion(bf16[320,40,128]{2,0,1:T(8,128)(2,1)} %pad_maximum_fusion, s32[1024]{0:T(1024)S(1)} %pad_clamp_fusion), kind=kCustom, calls=%fused_computation.7 | custom fusion | bytes 6553760 | tf_op jit(solution)/shard_map/jit(_take)/gather | solution.py:144
  208.2 4.3 %bitcast_select_fusion = bf16[320,5120]{1,0:T(8,128)(2,1)} fusion(pred[5120]{0:T(1024)(128)(4,1)S(1)} %broadcast_bitcast_fusion, bf16[40,320,128]{2,1,0:T(8,128)(2,1)} %gather_fusion.1), kind=kLoop, calls=%fused_computation.28 | loop fusion | flops 1638400 | bytes 6558720 | tf_op jit(solution)/shard_map/jit(_take)/select_n | solution.py:144
  (64 shorter events, 19.4 us)
Async XLA Ops:
  0.0 1.9 copy-start
  0.0 4.5 %copy-start.13 = (s32[40]{0:T(128)S(1)}, s32[40]{0:T(128)}, u32[]{:S(2)}) copy-start(s32[40]{0:T(128)} %param.14) | copy-start | bytes 484
  6.7 4.7 %copy-start.4 = (bf16[320,40,128]{2,0,1:T(8,128)(2,1)S(1)}, bf16[320,40,128]{2,0,1:T(8,128)(2,1)}, u32[]{:S(2)}) copy-start(bf16[320,40,128]{2,0,1:T(8,128)(2,1)} %copy_bitcast_fusion.1) | copy-start | bytes 9830404
  29.4 36.9 %all-to-all-start.2 = ((bf16[1,320,10,128]{3,2,0,1:T(8,128)(2,1)}), bf16[1,320,10,128]{3,2,0,1:T(8,128)(2,1)}, u32[]{:S(2)}, u32[]{:S(2)}) async-start(bf16[1,320,10,128]{3,2,0,1:T(8,128)(2,1)} %copy.97), calls=%async_computation.2 | async-start | bytes 2621440 | tf_op jit(solution)/shard_map/all_to_all | solution.py:60
  42.7 4.4 %copy-start.5 = (bf16[30,320,128]{2,1,0:T(8,128)(2,1)S(1)}, bf16[30,320,128]{2,1,0:T(8,128)(2,1)}, u32[]{:S(2)}) copy-start(bf16[30,320,128]{2,1,0:T(8,128)(2,1)} %gather_fusion.4) | copy-start | bytes 7372804
  53.3 23.9 %collective-permute-start = (bf16[320,15,128]{2,0,1:T(8,128)(2,1)}, bf16[320,15,128]{2,0,1:T(8,128)(2,1)}, u32[]{:S(2)}, u32[]{:S(2)}) collective-permute-start(bf16[320,15,128]{2,0,1:T(8,128)(2,1)} %get-tuple-element.157), channel_id=1, source_target_pairs={{0,1},{1,0},{2,3},{3,2},{4,5},{5,4},{6,7},{7,6},{8,9},{9,8},{10,11... | collective-permute-start | bytes 3686408 | tf_op jit(solution)/shard_map/ppermute | solution.py:17
  53.6 1.8 copy-start.11
  55.3 16.3 %copy-start.6 = (bf16[320,30,128]{2,0,1:T(8,128)(2,1)S(1)}, bf16[320,30,128]{2,0,1:T(8,128)(2,1)}, u32[]{:S(2)}) copy-start(bf16[320,30,128]{2,0,1:T(8,128)(2,1)} %get-tuple-element.158) | copy-start | bytes 7372804
  55.3 26.0 %collective-permute-start.1 = (bf16[320,15,128]{2,0,1:T(8,128)(2,1)}, bf16[320,15,128]{2,0,1:T(8,128)(2,1)}, u32[]{:S(2)}, u32[]{:S(2)}) collective-permute-start(bf16[320,15,128]{2,0,1:T(8,128)(2,1)} %get-tuple-element.155), channel_id=1, source_target_pairs={{0,1},{1,0},{2,3},{3,2},{4,5},{5,4},{6,7},{7,6},{8,9},{9,8},{10,11... | collective-permute-start | bytes 3686408 | tf_op jit(solution)/shard_map/ppermute | solution.py:17
  66.3 35.5 %all-to-all-start.1 = ((bf16[1,320,10,128]{3,2,0,1:T(8,128)(2,1)}), bf16[1,320,10,128]{3,2,0,1:T(8,128)(2,1)}, u32[]{:S(2)}, u32[]{:S(2)}) async-start(bf16[1,320,10,128]{3,2,0,1:T(8,128)(2,1)} %copy.94), calls=%async_computation.1 | async-start | bytes 2621440 | tf_op jit(solution)/shard_map/all_to_all | solution.py:59
  71.6 4.8 %copy-start.2 = (s32[40]{0:T(128)S(1)}, s32[40]{0:T(128)}, u32[]{:S(2)}) copy-start(s32[40]{0:T(128)} %param.15) | copy-start | bytes 484
  73.2 4.0 %copy-start.8 = (bf16[320,15,128]{2,0,1:T(8,128)(2,1)S(1)}, bf16[320,15,128]{2,0,1:T(8,128)(2,1)}, u32[]{:S(2)}) copy-start(bf16[320,15,128]{2,0,1:T(8,128)(2,1)} %get-tuple-element.156) | copy-start | bytes 3686404
  73.2 11.9 %collective-permute-start.2 = (bf16[320,15,128]{2,0,1:T(8,128)(2,1)}, bf16[320,15,128]{2,0,1:T(8,128)(2,1)}, u32[]{:S(2)}, u32[]{:S(2)}) collective-permute-start(bf16[320,15,128]{2,0,1:T(8,128)(2,1)} %get-tuple-element.153), channel_id=1, source_target_pairs={{0,1},{1,0},{2,3},{3,2},{4,5},{5,4},{6,7},{7,6},{8,9},{9,8},{10,11... | collective-permute-start | bytes 3686408 | tf_op jit(solution)/shard_map/ppermute | solution.py:17
  77.2 4.0 %copy-start.9 = (bf16[320,15,128]{2,0,1:T(8,128)(2,1)S(1)}, bf16[320,15,128]{2,0,1:T(8,128)(2,1)}, u32[]{:S(2)}) copy-start(bf16[320,15,128]{2,0,1:T(8,128)(2,1)} %get-tuple-element.154) | copy-start | bytes 3686404
  81.2 4.0 %copy-start.10 = (bf16[320,15,128]{2,0,1:T(8,128)(2,1)S(1)}, bf16[320,15,128]{2,0,1:T(8,128)(2,1)}, u32[]{:S(2)}) copy-start(bf16[320,15,128]{2,0,1:T(8,128)(2,1)} %get-tuple-element.152) | copy-start | bytes 3686404
  101.9 61.8 %all-to-all-start = ((bf16[1,320,10,128]{3,2,0,1:T(8,128)(2,1)}), bf16[1,320,10,128]{3,2,0,1:T(8,128)(2,1)S(1)}, u32[]{:S(2)}, u32[]{:S(2)}) async-start(bf16[1,320,10,128]{3,2,0,1:T(8,128)(2,1)} %copy.91), calls=%async_computation | async-start | bytes 2621440 | tf_op jit(solution)/shard_map/all_to_all | solution.py:61
  111.7 3.2 %copy-start.3 = (f32[5,640,640]{1,2,0:T(8,128)}, f32[5,640,640]{1,2,0:T(8,128)S(1)}, u32[]{:S(2)}) copy-start(f32[5,640,640]{1,2,0:T(8,128)S(1)} %fusion.48) | copy-start | bytes 24576004 | tf_op jit(solution)/shard_map/while
  128.4 3.2 %copy-start.3 = (f32[5,640,640]{1,2,0:T(8,128)}, f32[5,640,640]{1,2,0:T(8,128)S(1)}, u32[]{:S(2)}) copy-start(f32[5,640,640]{1,2,0:T(8,128)S(1)} %fusion.48) | copy-start | bytes 24576004 | tf_op jit(solution)/shard_map/while
  145.2 3.2 %copy-start.3 = (f32[5,640,640]{1,2,0:T(8,128)}, f32[5,640,640]{1,2,0:T(8,128)S(1)}, u32[]{:S(2)}) copy-start(f32[5,640,640]{1,2,0:T(8,128)S(1)} %fusion.48) | copy-start | bytes 24576004 | tf_op jit(solution)/shard_map/while
  165.5 8.6 %copy-start.7 = (bf16[640,15,128]{2,0,1:T(8,128)(2,1)S(1)}, bf16[640,15,128]{2,0,1:T(8,128)(2,1)}, u32[]{:S(2)}) copy-start(bf16[640,15,128]{2,0,1:T(8,128)(2,1)} %get-tuple-element.105) | copy-start | bytes 7372804
  168.0 29.6 %all-to-all-start.3 = ((bf16[16,20,10,128]{3,1,2,0:T(8,128)(2,1)}), bf16[16,20,10,128]{3,1,2,0:T(8,128)(2,1)}, u32[]{:S(2)}, u32[]{:S(2)}) async-start(bf16[16,20,10,128]{3,1,2,0:T(8,128)(2,1)} %copy.104), calls=%async_computation.3 | async-start | bytes 1966080 | tf_op jit(solution)/shard_map/all_to_all | solution.py:88
  175.7 3.1 %collective-permute-start.3 = (bf16[320,15,128]{2,0,1:T(8,128)(2,1)}, bf16[320,15,128]{2,0,1:T(8,128)(2,1)S(1)}, u32[]{:S(2)}, u32[]{:S(2)}) collective-permute-start(bf16[320,15,128]{2,0,1:T(8,128)(2,1)} %get-tuple-element.151), channel_id=1, source_target_pairs={{0,1},{1,0},{2,3},{3,2},{4,5},{5,4},{6,7},{7,6},{8,9},{9,8},{10,11... | collective-permute-start | bytes 3686408 | tf_op jit(solution)/shard_map/ppermute | solution.py:17
  178.8 1.0 copy-start.12
  203.3 9.2 %copy-start.1 = (bf16[320,5120]{1,0:T(8,128)(2,1)S(1)}, bf16[320,5120]{1,0:T(8,128)(2,1)}, u32[]{:S(2)}) copy-start(bf16[320,5120]{1,0:T(8,128)(2,1)} %param.11) | copy-start | bytes 9830404
where the time goes:
time: 213 us
  local copies, waits for them, and re-layouts  71.1 us (33%)
  matrix products  39.9 us (19%)
  other arithmetic  39.1 us (18%)
  waiting for transfers between devices  37.8 us (18%)
  starting transfers between devices  24.4 us (11%)
    dot_general x3, matrix products, one_block(): jnp.einsum('hrk,khd->rhd', weights, value_block, preferred_element_type=j...  26 us
    all_to_all x1, waiting for transfers between devices, attend_columns(): lax.all_to_all(output, 'frame', split_axis=0, concat_axis=1, tiled=True)  15.1 us
    all_to_all x1, waiting for transfers between devices, attend_columns(): lax.all_to_all(query_part[None], 'frame', split_axis=1, concat_axis=0, ti...  12.9 us
    select_n x3, other arithmetic, whole_frame(): jnp.where(parity == 0, jnp.concatenate([own, got], axis=0), jnp.concatena...  11.7 us
    all_to_all x1, waiting for transfers between devices, attend_columns(): lax.all_to_all(key_part[None], 'frame', split_axis=1, concat_axis=0, tile...  9.25 us
    dot_general x3, matrix products, one_block(): jnp.einsum('rhd,khd->hrk', query_block, key_block, preferred_element_type...  7.85 us
    dynamic_update_slice x6, local copies, waits for them, and re-layouts, one_block(): return lax.dynamic_update_slice_in_dim(result, output_block, start, 1)  7.02 us
    all_to_all x1, starting transfers between devices, attend_columns(): lax.all_to_all(key_part[None], 'frame', split_axis=1, concat_axis=0, tile...  6.61 us
  transfers between devices with their start and end apart: 8, of which 4 were waited for; matrix products, arithmetic and copies ran while one was open for 46% of the time, Pallas kernels for 0%

commit v1 on v0

--- a/solution.py
+++ b/solution.py
@@ -5,6 +5,18 @@
 from jax.sharding import PartitionSpec as P
 
 TEMP_HEADS = 10
+
+
+def in_blocks(x, dim, size):
+    shape = x.shape
+    tiles = x.reshape(*shape[:dim], size, shape[dim] // size, *shape[dim + 1 :])
+    return jnp.moveaxis(tiles, dim, 0)
+
+
+def laid_out(blocks, dim):
+    blocks = jnp.moveaxis(blocks, 0, dim)
+    shape = blocks.shape
+    return blocks.reshape(*shape[:dim], shape[dim] * shape[dim + 1], *shape[dim + 2 :])
 
 
 def from_partner(block, axis, bit):
@@ -85,7 +97,14 @@
         preferred_element_type=jnp.float32,
     ).astype(jnp.bfloat16)
     output = output.reshape(sources, pixels, head_part, head_size)
-    returned = lax.all_to_all(output, "frame", split_axis=0, concat_axis=1, tiled=True)
+    length, index = (lax.axis_size("frame"), lax.axis_index("frame"))
+    tiles = in_blocks(output, 0, length)
+    done = [tiles[index]]
+    for hop in range(1, length):
+        sent = tiles[index ^ hop]
+        done.append(lax.ppermute(sent, "frame", [(i, i ^ hop) for i in range(length)]))
+    tiles = jnp.stack(done)[index ^ jnp.arange(length)]
+    returned = laid_out(tiles, 1)
     return returned[0]
 
 

time: 213 us -> 220 us (1.033)
  starting transfers between devices: 24.4 us -> 35 us
  waiting for transfers between devices: 37.8 us -> 32.6 us
  local copies, waits for them, and re-layouts: 71.1 us -> 67.7 us
    ppermute x0 -> x15, starting transfers between devices: none -> 16.9 us  [attend_columns(): lax.ppermute(sent, 'frame', [(i, i ^ hop) for i in range(length)])]
    ppermute x0 -> x15, waiting for transfers between devices: none -> 15.3 us  [attend_columns(): lax.ppermute(sent, 'frame', [(i, i ^ hop) for i in range(length)])]
    all_to_all x1 -> x0, waiting for transfers between devices: 15.1 us -> none  [attend_columns(): lax.all_to_all(output, 'frame', split_axis=0, concat_axis=1, tiled=True)]
    all_to_all x1, waiting for transfers between devices: 9.25 us -> 1.54 us  [attend_columns(): lax.all_to_all(key_part[None], 'frame', split_axis=1, concat_axis=0, tile...]
    all_to_all x1 -> x0, starting transfers between devices: 6.02 us -> none  [attend_columns(): lax.all_to_all(output, 'frame', split_axis=0, concat_axis=1, tiled=True)]
    all_to_all x1, waiting for transfers between devices: 12.9 us -> 15.8 us  [attend_columns(): lax.all_to_all(query_part[None], 'frame', split_axis=1, concat_axis=0, ti...]
    all_to_all x1 -> x0, local copies, waits for them, and re-layouts: 2.36 us -> none  [attend_columns(): lax.all_to_all(output, 'frame', split_axis=0, concat_axis=1, tiled=True)]
  transfers between devices with their start and end apart: 8 -> 22, of which waited for: 4 -> 10; matrix products, arithmetic and copies ran while one was open for 46% -> 48% of each run, Pallas kernels for 0% -> 0%
where the time goes in v1:
time: 220 us; the launch traced here: 218 us
  local copies, waits for them, and re-layouts  67.7 us (31%)
  other arithmetic  41 us (19%)
  matrix products  40.8 us (19%)
  starting transfers between devices  35 us (16%)
  waiting for transfers between devices  32.6 us (15%)
    dot_general x3, matrix products, one_block(): jnp.einsum('hrk,khd->rhd', weights, value_block, preferred_element_type=j...  26 us
    ppermute x15, starting transfers between devices, attend_columns(): lax.ppermute(sent, 'frame', [(i, i ^ hop) for i in range(length)])  16.9 us
    all_to_all x1, waiting for transfers between devices, attend_columns(): lax.all_to_all(query_part[None], 'frame', split_axis=1, concat_axis=0, ti...  15.8 us
    ppermute x15, waiting for transfers between devices, attend_columns(): lax.ppermute(sent, 'frame', [(i, i ^ hop) for i in range(length)])  15.3 us
    select_n x3, other arithmetic, whole_frame(): jnp.where(parity == 0, jnp.concatenate([own, got], axis=0), jnp.concatena...  11.8 us
    dot_general x3, matrix products, one_block(): jnp.einsum('rhd,khd->hrk', query_block, key_block, preferred_element_type...  7.84 us
    dynamic_update_slice x6, local copies, waits for them, and re-layouts, one_block(): return lax.dynamic_update_slice_in_dim(result, output_block, start, 1)  7.02 us
    all_to_all x1, starting transfers between devices, attend_columns(): lax.all_to_all(key_part[None], 'frame', split_axis=1, concat_axis=0, tile...  6.61 us
  transfers between devices with their start and end apart: 22, of which 10 were waited for; matrix products, arithmetic and copies ran while one was open for 48% of the time, Pallas kernels for 0%

profile of v1, /device:TPU:9, one launch (start us, length us, event | category | flops | bytes accessed | tf_op | source)
XLA Modules:
  0.0 217.8 jit_solution(14193096866032544922)
XLA Ops:
  0.0 2.8 %sort.31 = (s32[40]{0:T(128)}, s32[40]{0:T(128)S(1)}) sort(s32[40]{0:T(128)} %param.14, s32[40]{0:T(128)S(1)} %iota.25), dimensions={0}, to_apply=%region_0.0 | sort | flops 240 | bytes 640 | tf_op jit(solution)/shard_map/jit(argsort)/sort | solution.py:119
  3.0 2.6 %copy_bitcast_fusion.1 = bf16[320,40,128]{2,0,1:T(8,128)(2,1)} fusion(bf16[320,5120]{1,0:T(8,128)(2,1)S(1)} %copy-done), kind=kLoop, calls=%fused_computation.31 | loop fusion | bytes 6553600 | tf_op jit(solution)/shard_map/reshape | solution.py:115
  5.6 2.6 %copy_bitcast_fusion = bf16[320,40,128]{2,0,1:T(8,128)(2,1)} fusion(bf16[320,5120]{1,0:T(8,128)(2,1)S(1)} %copy-done.13), kind=kLoop, calls=%fused_computation.30 | loop fusion | bytes 6553600 | tf_op jit(solution)/shard_map/reshape | solution.py:116
  9.8 3.5 %gather_fusion.8 = bf16[10,320,128]{2,1,0:T(8,128)(2,1)} fusion(bf16[320,40,128]{2,0,1:T(8,128)(2,1)} %copy_bitcast_fusion, s32[1024]{0:T(1024)S(1)} %get-tuple-element.177), kind=kCustom, calls=%fused_computation.5.clone | custom fusion | bytes 1638440 | tf_op jit(solution)/shard_map/jit(_take)/gather | solution.py:129
  13.3 4.5 %copy_bitcast_fusion.2 = bf16[320,40,128]{2,0,1:T(8,128)(2,1)} fusion(bf16[320,5120]{1,0:T(8,128)(2,1)} %param.13), kind=kLoop, calls=%fused_computation.32 | loop fusion | bytes 6553600 | tf_op jit(solution)/shard_map/reshape | solution.py:117
  17.8 3.5 %gather_fusion.6 = bf16[10,320,128]{2,1,0:T(8,128)(2,1)} fusion(bf16[320,40,128]{2,0,1:T(8,128)(2,1)} %copy_bitcast_fusion.2, s32[1024]{0:T(1024)S(1)} %get-tuple-element.177), kind=kCustom, calls=%fused_computation.1.clone | custom fusion | bytes 1638440 | tf_op jit(solution)/shard_map/jit(_take)/gather | solution.py:130
  21.4 3.1 %select_bitcast_fusion.4 = (bf16[1,320,10,128]{3,1,2,0:T(8,128)(2,1)}, bf16[1,320,10,128]{3,1,2,0:T(8,128)(2,1)S(1)}, bf16[1,320,10,128]{3,1,2,0:T(8,128)(2,1)}) fusion(bf16[10,320,128]{2,1,0:T(8,128)(2,1)} %gather_fusion.7, pred[10]{0:T(512)(128)(4,1)S(1)} %get-tuple-element.143, bf16[10,320,128]{2,1,0:T(8,128)(2,1)} %gather_fusion.8, ...), kind=kLoop, calls=%fused_computation.51 | loop fusion | flops 1228800 | bytes 4915210 | tf_op jit(solution)/shard_map/broadcast_in_dim | solution.py:71
  24.4 1.7 copy.120
  26.2 6.6 %all-to-all-start.2 = ((bf16[1,320,10,128]{3,2,0,1:T(8,128)(2,1)}), bf16[1,320,10,128]{3,2,0,1:T(8,128)(2,1)}, u32[]{:S(2)}, u32[]{:S(2)}) async-start(bf16[1,320,10,128]{3,2,0,1:T(8,128)(2,1)} %copy.120), calls=%async_computation.2 | async-start | bytes 2621440 | tf_op jit(solution)/shard_map/all_to_all | solution.py:72
  32.8 4.3 %gather_fusion.5 = bf16[30,320,128]{2,1,0:T(8,128)(2,1)} fusion(bf16[320,40,128]{2,0,1:T(8,128)(2,1)} %copy_bitcast_fusion, s32[1024]{0:T(1024)S(1)} %get-tuple-element.178), kind=kCustom, calls=%fused_computation.3.clone | custom fusion | bytes 4915320 | tf_op jit(solution)/shard_map/jit(_take)/gather | solution.py:124
  37.0 2.3 %gather_fusion.4 = bf16[30,320,128]{2,1,0:T(8,128)(2,1)} fusion(bf16[320,40,128]{2,0,1:T(8,128)(2,1)S(1)} %copy-done.4, s32[1024]{0:T(1024)S(1)} %get-tuple-element.178), kind=kCustom, calls=%fused_computation.2.clone | custom fusion | bytes 4915320 | tf_op jit(solution)/shard_map/jit(_take)/gather | solution.py:123
  39.4 4.4 %gather_fusion.3 = bf16[30,320,128]{2,1,0:T(8,128)(2,1)} fusion(bf16[320,40,128]{2,0,1:T(8,128)(2,1)} %copy_bitcast_fusion.2, s32[1024]{0:T(1024)S(1)} %get-tuple-element.178), kind=kCustom, calls=%fused_computation.clone | custom fusion | bytes 4915320 | tf_op jit(solution)/shard_map/jit(_take)/gather | solution.py:125
  43.8 5.8 %select_bitcast_fusion = (bf16[320,30,128]{2,0,1:T(8,128)(2,1)}, bf16[320,30,128]{2,0,1:T(8,128)(2,1)}, bf16[320,30,128]{2,0,1:T(8,128)(2,1)}) fusion(bf16[30,320,128]{2,1,0:T(8,128)(2,1)S(1)} %copy-done.5, pred[30]{0:T(512)(128)(4,1)S(1)} %get-tuple-element.141, bf16[30,320,128]{2,1,0:T(8,128)(2,1)} %gather_fusion.4, bf16[30,320,128]{2,1,0:T(8,128)(2,1)} %gather_fusion.3), kind=kLoop, calls=%fused_computation.38 | loop fusion | flops 3686400 | bytes 14745630 | tf_op jit(solution)/shard_map/jit(_take)/select_n | solution.py:124
  49.6 3.4 %constant_dynamic-slice_fusion.23 = (bf16[320,15,128]{2,0,1:T(8,128)(2,1)}, bf16[320,15,128]{2,0,1:T(8,128)(2,1)}) fusion(bf16[320,30,128]{2,0,1:T(8,128)(2,1)} %get-tuple-element.171, s32[]{:T(128)S(6)} %select_n.157, s32[]{:T(128)S(6)} %select_n.158), kind=kLoop, calls=%fused_computation.109 | loop fusion | bytes 4915208 | tf_op jit(solution)/shard_map/dynamic_slice | solution.py:139
  57.8 2.0 sort.32
  59.8 1.6 copy.117
  63.1 5.2 %all-to-all-start.1 = ((bf16[1,320,10,128]{3,2,0,1:T(8,128)(2,1)}), bf16[1,320,10,128]{3,2,0,1:T(8,128)(2,1)}, u32[]{:S(2)}, u32[]{:S(2)}) async-start(bf16[1,320,10,128]{3,2,0,1:T(8,128)(2,1)} %copy.117), calls=%async_computation.1 | async-start | bytes 2621440 | tf_op jit(solution)/shard_map/all_to_all | solution.py:71
  71.0 4.0 %maximum_select_fusion = bf16[640,15,128]{2,0,1:T(8,128)(2,1)} fusion(bf16[320,15,128]{2,0,1:T(8,128)(2,1)} %collective-permute-done, bf16[320,15,128]{2,0,1:T(8,128)(2,1)S(1)} %copy-done.8, pred[]{:T(512)S(6)} %eq.4), kind=kLoop, calls=%fused_computation.34 | loop fusion | flops 11059200 | bytes 4915201 | tf_op jit(solution)/shard_map/jit(_where)/select_n | solution.py:146
  75.0 4.0 %maximum_select_fusion.1 = bf16[640,15,128]{2,0,1:T(8,128)(2,1)} fusion(bf16[320,15,128]{2,0,1:T(8,128)(2,1)} %collective-permute-done.1, bf16[320,15,128]{2,0,1:T(8,128)(2,1)S(1)} %copy-done.9, pred[]{:T(512)S(6)} %eq.4), kind=kLoop, calls=%fused_computation.35 | loop fusion | flops 11059200 | bytes 4915201 | tf_op jit(solution)/shard_map/jit(_where)/select_n | solution.py:146
  79.0 3.8 %maximum_select_fusion.2 = bf16[640,15,128]{2,0,1:T(8,128)(2,1)} fusion(bf16[320,15,128]{2,0,1:T(8,128)(2,1)} %collective-permute-done.2, bf16[320,15,128]{2,0,1:T(8,128)(2,1)S(1)} %copy-done.10, pred[]{:T(512)S(6)} %eq.4), kind=kLoop, calls=%fused_computation.36 | loop fusion | flops 11059200 | bytes 4915201 | tf_op jit(solution)/shard_map/jit(_where)/select_n | solution.py:146
  82.8 15.8 %all-to-all-done.1 = bf16[1,320,10,128]{3,2,0,1:T(8,128)(2,1)} async-done(((bf16[1,320,10,128]{3,2,0,1:T(8,128)(2,1)}), bf16[1,320,10,128]{3,2,0,1:T(8,128)(2,1)}, u32[]{:S(2)}, u32[]{:S(2)}) %all-to-all-start.1) | async-done | bytes 819232 | tf_op jit(solution)/shard_map/all_to_all | solution.py:71
  98.6 5.3 %all-to-all-start = ((bf16[1,320,10,128]{3,2,0,1:T(8,128)(2,1)}), bf16[1,320,10,128]{3,2,0,1:T(8,128)(2,1)S(1)}, u32[]{:S(2)}, u32[]{:S(2)}) async-start(bf16[1,320,10,128]{3,2,0,1:T(8,128)(2,1)} %copy.114), calls=%async_computation | async-start | bytes 2621440 | tf_op jit(solution)/shard_map/all_to_all | solution.py:73
  103.8 1.9 broadcast_in_dim.74.clone
  105.8 50.4 %while.13 = (s32[]{:T(128)}, bf16[640,15,128]{2,0,1:T(8,128)(2,1)}, bf16[640,15,128]{2,0,1:T(8,128)(2,1)}, bf16[640,15,128]{2,0,1:T(8,128)(2,1)}, bf16[640,15,12...) while((s32[]{:T(128)}, bf16[640,15,128]{2,0,1:T(8,128)(2,1)}, ...), condition=%wide.region_5.7_spmd, body=%wide.region_2.6_spmd.sunk | while | flops 1067422080 | bytes 72116400 | solution.py:66
  105.8 2.6 %fusion.49 = f32[5,640,640]{1,2,0:T(8,128)S(1)} fusion(bf16[640,15,128]{2,0,1:T(8,128)(2,1)} %get-tuple-element.232, s32[]{:T(128)S(6)} %select_n.242, bf16[640,15,128]{2,0,1:T(8,128)(2,1)} %get-tuple-element.231), kind=kOutput, calls=%fused_computation.18.clone.1 | convolution fusion | flops 524288000 | bytes 9831424 | tf_op jit(solution)/shard_map/while/body/eval_jaxpr/rhd,khd->hrk/dot_general | solution.py:56
  108.4 2.1 fusion.50
  111.6 8.7 %fusion.51 = bf16[640,5,128]{0,2,1:T(8,128)(2,1)S(1)} fusion(f32[5,640]{1,0:T(8,128)S(1)} %fusion.50, bf16[640,15,128]{2,0,1:T(8,128)(2,1)} %get-tuple-element.230, s32[]{:T(128)S(6)} %select_n.242, f32[5,640,640]{1,2,0:T(8,128)} %copy-done.3), kind=kOutput, calls=%fused_computation.17.clone.1 | convolution fusion | flops 534941440 | bytes 18035204 | tf_op jit(solution)/shard_map/while/body/eval_jaxpr/hrk,khd->rhd/dot_general | solution.py:60
  122.6 2.6 %fusion.49 = f32[5,640,640]{1,2,0:T(8,128)S(1)} fusion(bf16[640,15,128]{2,0,1:T(8,128)(2,1)} %get-tuple-element.232, s32[]{:T(128)S(6)} %select_n.242, bf16[640,15,128]{2,0,1:T(8,128)(2,1)} %get-tuple-element.231), kind=kOutput, calls=%fused_computation.18.clone.1 | convolution fusion | flops 524288000 | bytes 9831424 | tf_op jit(solution)/shard_map/while/body/eval_jaxpr/rhd,khd->hrk/dot_general | solution.py:56
  125.2 2.1 fusion.50
  128.4 8.7 %fusion.51 = bf16[640,5,128]{0,2,1:T(8,128)(2,1)S(1)} fusion(f32[5,640]{1,0:T(8,128)S(1)} %fusion.50, bf16[640,15,128]{2,0,1:T(8,128)(2,1)} %get-tuple-element.230, s32[]{:T(128)S(6)} %select_n.242, f32[5,640,640]{1,2,0:T(8,128)} %copy-done.3), kind=kOutput, calls=%fused_computation.17.clone.1 | convolution fusion | flops 534941440 | bytes 18035204 | tf_op jit(solution)/shard_map/while/body/eval_jaxpr/hrk,khd->rhd/dot_general | solution.py:60
  139.4 2.6 %fusion.49 = f32[5,640,640]{1,2,0:T(8,128)S(1)} fusion(bf16[640,15,128]{2,0,1:T(8,128)(2,1)} %get-tuple-element.232, s32[]{:T(128)S(6)} %select_n.242, bf16[640,15,128]{2,0,1:T(8,128)(2,1)} %get-tuple-element.231), kind=kOutput, calls=%fused_computation.18.clone.1 | convolution fusion | flops 524288000 | bytes 9831424 | tf_op jit(solution)/shard_map/while/body/eval_jaxpr/rhd,khd->hrk/dot_general | solution.py:56
  142.0 2.1 fusion.50
  145.2 8.7 %fusion.51 = bf16[640,5,128]{0,2,1:T(8,128)(2,1)S(1)} fusion(f32[5,640]{1,0:T(8,128)S(1)} %fusion.50, bf16[640,15,128]{2,0,1:T(8,128)(2,1)} %get-tuple-element.230, s32[]{:T(128)S(6)} %select_n.242, f32[5,640,640]{1,2,0:T(8,128)} %copy-done.3), kind=kOutput, calls=%fused_computation.17.clone.1 | convolution fusion | flops 534941440 | bytes 18035204 | tf_op jit(solution)/shard_map/while/body/eval_jaxpr/hrk,khd->rhd/dot_general | solution.py:60
  156.2 3.3 %constant_dynamic-slice_fusion.17 = (bf16[320,15,128]{2,0,1:T(8,128)(2,1)}, bf16[320,15,128]{2,0,1:T(8,128)(2,1)}) fusion(bf16[640,15,128]{2,0,1:T(8,128)(2,1)} %get-tuple-element.105, s32[]{:T(128)S(6)} %select_n.162, s32[]{:T(128)S(6)} %select_n.163), kind=kLoop, calls=%fused_computation.103 | loop fusion | bytes 4915208 | tf_op jit(solution)/shard_map/dynamic_slice | solution.py:155
  159.8 4.6 %exponential_reduce_fusion = (f32[2,20,10,8]{3,2,1,0:T(8,128)S(1)}, f32[2,20,10,8,8]{3,4,2,1,0:T(8,128)}) fusion(bf16[8,2,20,10,128]{4,3,2,1,0:T(8,128)(2,1)} %bitcast.13, bf16[8,2,20,10,128]{4,3,2,1,0:T(8,128)(2,1)} %bitcast.10, pred[10,8,8]{1,2,0:T(8,128)(4,1)S(1)} %broadcast_compare_fusion), kind=kOutput, calls=%fused_computation.44 | convolution fusion | flops 6656007 | bytes 1754240 | tf_op jit(solution)/shard_map/sub | solution.py:34
  164.5 2.3 %fusion.24 = bf16[8,2,20,10,128]{4,0,3,2,1:T(8,128)(2,1)S(1)} fusion(bf16[8,2,20,10,128]{4,3,2,1,0:T(8,128)(2,1)S(1)} %bitcast.133, f32[2,20,10,8,8]{3,4,2,1,0:T(8,128)} %get-tuple-element.176, f32[2,20,10,8]{3,2,1,0:T(8,128)S(1)} %get-tuple-element.175), kind=kOutput, calls=%fused_computation.46 | convolution fusion | flops 7014400 | bytes 1753600 | tf_op jit(solution)/shard_map/apnfg,gapnd->fapnd/dot_general | solution.py:93
  168.1 1.9 constant_dynamic-slice_fusion
  177.6 2.1 collective-permute-start.11
  180.0 3.1 %collective-permute-start.13 = (bf16[1,20,10,128]{3,1,2,0:T(8,128)(2,1)S(1)}, bf16[1,20,10,128]{3,1,2,0:T(8,128)(2,1)S(1)}, u32[]{:S(2)}, u32[]{:S(2)}) collective-permute-start(bf16[1,20,10,128]{3,1,2,0:T(8,128)(2,1)S(1)} %bitcast.139), channel_id=1, source_target_pairs={{0,10},{1,11},{2,8},{3,9},{4,14},{5,15},{6,12},{7,13},{8,2},{9,3},... | collective-permute-start | bytes 153608 | tf_op jit(solution)/shard_map/ppermute | solution.py:105
  185.5 2.5 %collective-permute-done.12 = bf16[1,20,10,128]{3,1,2,0:T(8,128)(2,1)S(1)} collective-permute-done((bf16[1,20,10,128]{3,1,2,0:T(8,128)(2,1)S(1)}, bf16[1,20,10,128]{3,1,2,0:T(8,128)(2,1)S(1)}, u32[]{:S(2)}, u32[]{:S(2)}) %collective-permute-start.12) | collective-permute-done | bytes 51232 | tf_op jit(solution)/shard_map/ppermute | solution.py:105
  188.0 1.8 collective-permute-done.13
  194.4 2.5 %collective-permute-done.16 = bf16[1,20,10,128]{3,1,2,0:T(8,128)(2,1)S(1)} collective-permute-done((bf16[1,20,10,128]{3,1,2,0:T(8,128)(2,1)S(1)}, bf16[1,20,10,128]{3,1,2,0:T(8,128)(2,1)S(1)}, u32[]{:S(2)}, u32[]{:S(2)}) %collective-permute-start.16) | collective-permute-done | bytes 51232 | tf_op jit(solution)/shard_map/ppermute | solution.py:105
  196.9 3.2 %collective-permute-done.17 = bf16[1,20,10,128]{3,1,2,0:T(8,128)(2,1)S(1)} collective-permute-done((bf16[1,20,10,128]{3,1,2,0:T(8,128)(2,1)S(1)}, bf16[1,20,10,128]{3,1,2,0:T(8,128)(2,1)S(1)}, u32[]{:S(2)}, u32[]{:S(2)}) %collective-permute-start.17) | collective-permute-done | bytes 51232 | tf_op jit(solution)/shard_map/ppermute | solution.py:105
  200.2 2.6 %collective-permute-done.18 = bf16[1,20,10,128]{3,1,2,0:T(8,128)(2,1)S(1)} collective-permute-done((bf16[1,20,10,128]{3,1,2,0:T(8,128)(2,1)S(1)}, bf16[1,20,10,128]{3,1,2,0:T(8,128)(2,1)S(1)}, u32[]{:S(2)}, u32[]{:S(2)}) %collective-permute-start.18) | collective-permute-done | bytes 51232 | tf_op jit(solution)/shard_map/ppermute | solution.py:105
  203.9 2.6 %maximum_select_fusion.3 = bf16[320,30,128]{2,0,1:T(8,128)(2,1)S(1)} fusion(bf16[320,15,128]{2,0,1:T(8,128)(2,1)} %collective-permute-done.3, bf16[320,15,128]{2,0,1:T(8,128)(2,1)} %get-tuple-element.145, pred[]{:T(512)S(6)} %eq.4), kind=kLoop, calls=%fused_computation.37 | loop fusion | flops 3686400 | bytes 4915201 | tf_op jit(solution)/shard_map/jit(_where)/select_n | solution.py:158
  206.6 2.0 pad_maximum_fusion
  208.6 4.9 %gather_fusion.2 = bf16[40,320,128]{2,1,0:T(8,128)(2,1)} fusion(bf16[320,40,128]{2,0,1:T(8,128)(2,1)} %pad_maximum_fusion, s32[1024]{0:T(1024)S(1)} %pad_clamp_fusion), kind=kCustom, calls=%fused_computation.8 | custom fusion | bytes 6553760 | tf_op jit(solution)/shard_map/jit(_take)/gather | solution.py:163
  213.5 4.3 %bitcast_select_fusion = bf16[320,5120]{1,0:T(8,128)(2,1)} fusion(pred[5120]{0:T(1024)(128)(4,1)S(1)} %broadcast_bitcast_fusion, bf16[40,320,128]{2,1,0:T(8,128)(2,1)} %gather_fusion.2), kind=kLoop, calls=%fused_computation.29 | loop fusion | flops 1638400 | bytes 6558720 | tf_op jit(solution)/shard_map/jit(_take)/select_n | solution.py:163
  (125 shorter events, 38.2 us)
Async XLA Ops:
  0.0 2.9 %copy-start = (bf16[320,5120]{1,0:T(8,128)(2,1)S(1)}, bf16[320,5120]{1,0:T(8,128)(2,1)}, u32[]{:S(2)}) copy-start(bf16[320,5120]{1,0:T(8,128)(2,1)} %param.11) | copy-start | bytes 9830404
  2.9 2.6 %copy-start.13 = (bf16[320,5120]{1,0:T(8,128)(2,1)S(1)}, bf16[320,5120]{1,0:T(8,128)(2,1)}, u32[]{:S(2)}) copy-start(bf16[320,5120]{1,0:T(8,128)(2,1)} %param.12) | copy-start | bytes 9830404
  5.6 2.6 %copy-start.4 = (bf16[320,40,128]{2,0,1:T(8,128)(2,1)S(1)}, bf16[320,40,128]{2,0,1:T(8,128)(2,1)}, u32[]{:S(2)}) copy-start(bf16[320,40,128]{2,0,1:T(8,128)(2,1)} %copy_bitcast_fusion.1) | copy-start | bytes 9830404
  26.2 36.9 %all-to-all-start.2 = ((bf16[1,320,10,128]{3,2,0,1:T(8,128)(2,1)}), bf16[1,320,10,128]{3,2,0,1:T(8,128)(2,1)}, u32[]{:S(2)}, u32[]{:S(2)}) async-start(bf16[1,320,10,128]{3,2,0,1:T(8,128)(2,1)} %copy.120), calls=%async_computation.2 | async-start | bytes 2621440 | tf_op jit(solution)/shard_map/all_to_all | solution.py:72
  39.4 4.4 %copy-start.5 = (bf16[30,320,128]{2,1,0:T(8,128)(2,1)S(1)}, bf16[30,320,128]{2,1,0:T(8,128)(2,1)}, u32[]{:S(2)}) copy-start(bf16[30,320,128]{2,1,0:T(8,128)(2,1)} %gather_fusion.5) | copy-start | bytes 7372804
  49.6 3.8 %copy-start.7 = (bf16[320,30,128]{2,0,1:T(8,128)(2,1)S(1)}, bf16[320,30,128]{2,0,1:T(8,128)(2,1)}, u32[]{:S(2)}) copy-start(bf16[320,30,128]{2,0,1:T(8,128)(2,1)} %get-tuple-element.170) | copy-start | bytes 7372804
  53.1 17.9 %collective-permute-start = (bf16[320,15,128]{2,0,1:T(8,128)(2,1)}, bf16[320,15,128]{2,0,1:T(8,128)(2,1)}, u32[]{:S(2)}, u32[]{:S(2)}) collective-permute-start(bf16[320,15,128]{2,0,1:T(8,128)(2,1)} %get-tuple-element.152), channel_id=1, source_target_pairs={{0,1},{1,0},{2,3},{3,2},{4,5},{5,4},{6,7},{7,6},{8,9},{9,8},{10,11... | collective-permute-start | bytes 3686408 | tf_op jit(solution)/shard_map/ppermute | solution.py:29
  53.4 2.6 %copy-start.6 = (bf16[320,30,128]{2,0,1:T(8,128)(2,1)S(1)}, bf16[320,30,128]{2,0,1:T(8,128)(2,1)}, u32[]{:S(2)}) copy-start(bf16[320,30,128]{2,0,1:T(8,128)(2,1)} %get-tuple-element.169) | copy-start | bytes 7372804
  55.0 20.0 %collective-permute-start.1 = (bf16[320,15,128]{2,0,1:T(8,128)(2,1)}, bf16[320,15,128]{2,0,1:T(8,128)(2,1)}, u32[]{:S(2)}, u32[]{:S(2)}) collective-permute-start(bf16[320,15,128]{2,0,1:T(8,128)(2,1)} %get-tuple-element.150), channel_id=1, source_target_pairs={{0,1},{1,0},{2,3},{3,2},{4,5},{5,4},{6,7},{7,6},{8,9},{9,8},{10,11... | collective-permute-start | bytes 3686408 | tf_op jit(solution)/shard_map/ppermute | solution.py:29
  56.0 3.8 %copy-start.12 = (bf16[1,320,10,128]{3,1,2,0:T(8,128)(2,1)S(1)}, bf16[1,320,10,128]{3,1,2,0:T(8,128)(2,1)}, u32[]{:S(2)}) copy-start(bf16[1,320,10,128]{3,1,2,0:T(8,128)(2,1)} %get-tuple-element.172) | copy-start | bytes 2457604
  57.6 10.8 %copy-start.11 = (bf16[1,320,10,128]{3,1,2,0:T(8,128)(2,1)S(1)}, bf16[1,320,10,128]{3,1,2,0:T(8,128)(2,1)}, u32[]{:S(2)}) copy-start(bf16[1,320,10,128]{3,1,2,0:T(8,128)(2,1)} %get-tuple-element.174) | copy-start | bytes 2457604
  57.6 21.4 %collective-permute-start.2 = (bf16[320,15,128]{2,0,1:T(8,128)(2,1)}, bf16[320,15,128]{2,0,1:T(8,128)(2,1)}, u32[]{:S(2)}, u32[]{:S(2)}) collective-permute-start(bf16[320,15,128]{2,0,1:T(8,128)(2,1)} %get-tuple-element.148), channel_id=1, source_target_pairs={{0,1},{1,0},{2,3},{3,2},{4,5},{5,4},{6,7},{7,6},{8,9},{9,8},{10,11... | collective-permute-start | bytes 3686408 | tf_op jit(solution)/shard_map/ppermute | solution.py:29
  61.4 8.6 %copy-start.2 = (s32[40]{0:T(128)S(1)}, s32[40]{0:T(128)}, u32[]{:S(2)}) copy-start(s32[40]{0:T(128)} %param.15) | copy-start | bytes 484
  61.5 9.5 %copy-start.8 = (bf16[320,15,128]{2,0,1:T(8,128)(2,1)S(1)}, bf16[320,15,128]{2,0,1:T(8,128)(2,1)}, u32[]{:S(2)}) copy-start(bf16[320,15,128]{2,0,1:T(8,128)(2,1)} %get-tuple-element.151) | copy-start | bytes 3686404
  63.1 35.5 %all-to-all-start.1 = ((bf16[1,320,10,128]{3,2,0,1:T(8,128)(2,1)}), bf16[1,320,10,128]{3,2,0,1:T(8,128)(2,1)}, u32[]{:S(2)}, u32[]{:S(2)}) async-start(bf16[1,320,10,128]{3,2,0,1:T(8,128)(2,1)} %copy.117), calls=%async_computation.1 | async-start | bytes 2621440 | tf_op jit(solution)/shard_map/all_to_all | solution.py:71
  71.0 4.0 %copy-start.9 = (bf16[320,15,128]{2,0,1:T(8,128)(2,1)S(1)}, bf16[320,15,128]{2,0,1:T(8,128)(2,1)}, u32[]{:S(2)}) copy-start(bf16[320,15,128]{2,0,1:T(8,128)(2,1)} %get-tuple-element.149) | copy-start | bytes 3686404
  75.0 4.0 %copy-start.10 = (bf16[320,15,128]{2,0,1:T(8,128)(2,1)S(1)}, bf16[320,15,128]{2,0,1:T(8,128)(2,1)}, u32[]{:S(2)}) copy-start(bf16[320,15,128]{2,0,1:T(8,128)(2,1)} %get-tuple-element.147) | copy-start | bytes 3686404
  98.6 65.9 %all-to-all-start = ((bf16[1,320,10,128]{3,2,0,1:T(8,128)(2,1)}), bf16[1,320,10,128]{3,2,0,1:T(8,128)(2,1)S(1)}, u32[]{:S(2)}, u32[]{:S(2)}) async-start(bf16[1,320,10,128]{3,2,0,1:T(8,128)(2,1)} %copy.114), calls=%async_computation | async-start | bytes 2621440 | tf_op jit(solution)/shard_map/all_to_all | solution.py:73
  108.4 3.2 %copy-start.3 = (f32[5,640,640]{1,2,0:T(8,128)}, f32[5,640,640]{1,2,0:T(8,128)S(1)}, u32[]{:S(2)}) copy-start(f32[5,640,640]{1,2,0:T(8,128)S(1)} %fusion.49) | copy-start | bytes 24576004 | tf_op jit(solution)/shard_map/while
  125.2 3.2 %copy-start.3 = (f32[5,640,640]{1,2,0:T(8,128)}, f32[5,640,640]{1,2,0:T(8,128)S(1)}, u32[]{:S(2)}) copy-start(f32[5,640,640]{1,2,0:T(8,128)S(1)} %fusion.49) | copy-start | bytes 24576004 | tf_op jit(solution)/shard_map/while
  142.0 3.2 %copy-start.3 = (f32[5,640,640]{1,2,0:T(8,128)}, f32[5,640,640]{1,2,0:T(8,128)S(1)}, u32[]{:S(2)}) copy-start(f32[5,640,640]{1,2,0:T(8,128)S(1)} %fusion.49) | copy-start | bytes 24576004 | tf_op jit(solution)/shard_map/while
  159.5 44.5 %collective-permute-start.3 = (bf16[320,15,128]{2,0,1:T(8,128)(2,1)}, bf16[320,15,128]{2,0,1:T(8,128)(2,1)}, u32[]{:S(2)}, u32[]{:S(2)}) collective-permute-start(bf16[320,15,128]{2,0,1:T(8,128)(2,1)} %get-tuple-element.146), channel_id=1, source_target_pairs={{0,1},{1,0},{2,3},{3,2},{4,5},{5,4},{6,7},{7,6},{8,9},{9,8},{10,11... | collective-permute-start | bytes 3686408 | tf_op jit(solution)/shard_map/ppermute | solution.py:29
  170.0 2.7 %collective-permute-start.4 = (bf16[1,20,10,128]{3,1,2,0:T(8,128)(2,1)S(1)}, bf16[1,20,10,128]{3,1,2,0:T(8,128)(2,1)S(1)}, u32[]{:S(2)}, u32[]{:S(2)}) collective-permute-start(bf16[1,20,10,128]{3,1,2,0:T(8,128)(2,1)S(1)} %bitcast.148), channel_id=1, source_target_pairs={{0,1},{1,0},{2,3},{3,2},{4,5},{5,4},{6,7},{7,6},{8,9},{9,8},{10,11... | collective-permute-start | bytes 153608 | tf_op jit(solution)/shard_map/ppermute | solution.py:105
  170.3 4.1 %collective-permute-start.5 = (bf16[1,20,10,128]{3,1,2,0:T(8,128)(2,1)S(1)}, bf16[1,20,10,128]{3,1,2,0:T(8,128)(2,1)S(1)}, u32[]{:S(2)}, u32[]{:S(2)}) collective-permute-start(bf16[1,20,10,128]{3,1,2,0:T(8,128)(2,1)S(1)} %bitcast.147), channel_id=1, source_target_pairs={{0,2},{1,3},{2,0},{3,1},{4,6},{5,7},{6,4},{7,5},{8,10},{9,11},{10,... | collective-permute-start | bytes 153608 | tf_op jit(solution)/shard_map/ppermute | solution.py:105
  171.5 4.6 %collective-permute-start.6 = (bf16[1,20,10,128]{3,1,2,0:T(8,128)(2,1)S(1)}, bf16[1,20,10,128]{3,1,2,0:T(8,128)(2,1)S(1)}, u32[]{:S(2)}, u32[]{:S(2)}) collective-permute-start(bf16[1,20,10,128]{3,1,2,0:T(8,128)(2,1)S(1)} %bitcast.146), channel_id=1, source_target_pairs={{0,3},{1,2},{2,1},{3,0},{4,7},{5,6},{6,5},{7,4},{8,11},{9,10},{10,... | collective-permute-start | bytes 153608 | tf_op jit(solution)/shard_map/ppermute | solution.py:105
  172.4 5.1 %collective-permute-start.7 = (bf16[1,20,10,128]{3,1,2,0:T(8,128)(2,1)S(1)}, bf16[1,20,10,128]{3,1,2,0:T(8,128)(2,1)S(1)}, u32[]{:S(2)}, u32[]{:S(2)}) collective-permute-start(bf16[1,20,10,128]{3,1,2,0:T(8,128)(2,1)S(1)} %bitcast.145), channel_id=1, source_target_pairs={{0,4},{1,5},{2,6},{3,7},{4,0},{5,1},{6,2},{7,3},{8,12},{9,13},{10,... | collective-permute-start | bytes 153608 | tf_op jit(solution)/shard_map/ppermute | solution.py:105
  172.8 7.0 %collective-permute-start.8 = (bf16[1,20,10,128]{3,1,2,0:T(8,128)(2,1)S(1)}, bf16[1,20,10,128]{3,1,2,0:T(8,128)(2,1)S(1)}, u32[]{:S(2)}, u32[]{:S(2)}) collective-permute-start(bf16[1,20,10,128]{3,1,2,0:T(8,128)(2,1)S(1)} %bitcast.144), channel_id=1, source_target_pairs={{0,5},{1,4},{2,7},{3,6},{4,1},{5,0},{6,3},{7,2},{8,13},{9,12},{10,... | collective-permute-start | bytes 153608 | tf_op jit(solution)/shard_map/ppermute | solution.py:105
  174.3 5.6 %collective-permute-start.9 = (bf16[1,20,10,128]{3,1,2,0:T(8,128)(2,1)S(1)}, bf16[1,20,10,128]{3,1,2,0:T(8,128)(2,1)S(1)}, u32[]{:S(2)}, u32[]{:S(2)}) collective-permute-start(bf16[1,20,10,128]{3,1,2,0:T(8,128)(2,1)S(1)} %bitcast.143), channel_id=1, source_target_pairs={{0,6},{1,7},{2,4},{3,5},{4,2},{5,3},{6,0},{7,1},{8,14},{9,15},{10,... | collective-permute-start | bytes 153608 | tf_op jit(solution)/shard_map/ppermute | solution.py:105
  176.2 6.9 %collective-permute-start.10 = (bf16[1,20,10,128]{3,1,2,0:T(8,128)(2,1)S(1)}, bf16[1,20,10,128]{3,1,2,0:T(8,128)(2,1)S(1)}, u32[]{:S(2)}, u32[]{:S(2)}) collective-permute-start(bf16[1,20,10,128]{3,1,2,0:T(8,128)(2,1)S(1)} %bitcast.142), channel_id=1, source_target_pairs={{0,7},{1,6},{2,5},{3,4},{4,3},{5,2},{6,1},{7,0},{8,15},{9,14},{10,... | collective-permute-start | bytes 153608 | tf_op jit(solution)/shard_map/ppermute | solution.py:105
  177.6 6.6 %collective-permute-start.11 = (bf16[1,20,10,128]{3,1,2,0:T(8,128)(2,1)S(1)}, bf16[1,20,10,128]{3,1,2,0:T(8,128)(2,1)S(1)}, u32[]{:S(2)}, u32[]{:S(2)}) collective-permute-start(bf16[1,20,10,128]{3,1,2,0:T(8,128)(2,1)S(1)} %bitcast.141), channel_id=1, source_target_pairs={{0,8},{1,9},{2,10},{3,11},{4,12},{5,13},{6,14},{7,15},{8,0},{9,1},... | collective-permute-start | bytes 153608 | tf_op jit(solution)/shard_map/ppermute | solution.py:105
  179.7 8.2 %collective-permute-start.12 = (bf16[1,20,10,128]{3,1,2,0:T(8,128)(2,1)S(1)}, bf16[1,20,10,128]{3,1,2,0:T(8,128)(2,1)S(1)}, u32[]{:S(2)}, u32[]{:S(2)}) collective-permute-start(bf16[1,20,10,128]{3,1,2,0:T(8,128)(2,1)S(1)} %bitcast.140), channel_id=1, source_target_pairs={{0,9},{1,8},{2,11},{3,10},{4,13},{5,12},{6,15},{7,14},{8,1},{9,0},... | collective-permute-start | bytes 153608 | tf_op jit(solution)/shard_map/ppermute | solution.py:105
  180.0 9.8 %collective-permute-start.13 = (bf16[1,20,10,128]{3,1,2,0:T(8,128)(2,1)S(1)}, bf16[1,20,10,128]{3,1,2,0:T(8,128)(2,1)S(1)}, u32[]{:S(2)}, u32[]{:S(2)}) collective-permute-start(bf16[1,20,10,128]{3,1,2,0:T(8,128)(2,1)S(1)} %bitcast.139), channel_id=1, source_target_pairs={{0,10},{1,11},{2,8},{3,9},{4,14},{5,15},{6,12},{7,13},{8,2},{9,3},... | collective-permute-start | bytes 153608 | tf_op jit(solution)/shard_map/ppermute | solution.py:105
  183.1 8.7 %collective-permute-start.14 = (bf16[1,20,10,128]{3,1,2,0:T(8,128)(2,1)S(1)}, bf16[1,20,10,128]{3,1,2,0:T(8,128)(2,1)S(1)}, u32[]{:S(2)}, u32[]{:S(2)}) collective-permute-start(bf16[1,20,10,128]{3,1,2,0:T(8,128)(2,1)S(1)} %bitcast.138), channel_id=1, source_target_pairs={{0,11},{1,10},{2,9},{3,8},{4,15},{5,14},{6,13},{7,12},{8,3},{9,2},... | collective-permute-start | bytes 153608 | tf_op jit(solution)/shard_map/ppermute | solution.py:105
  184.2 10.2 %collective-permute-start.15 = (bf16[1,20,10,128]{3,1,2,0:T(8,128)(2,1)S(1)}, bf16[1,20,10,128]{3,1,2,0:T(8,128)(2,1)S(1)}, u32[]{:S(2)}, u32[]{:S(2)}) collective-permute-start(bf16[1,20,10,128]{3,1,2,0:T(8,128)(2,1)S(1)} %bitcast.137), channel_id=1, source_target_pairs={{0,12},{1,13},{2,14},{3,15},{4,8},{5,9},{6,10},{7,11},{8,4},{9,5},... | collective-permute-start | bytes 153608 | tf_op jit(solution)/shard_map/ppermute | solution.py:105
  187.9 9.0 %collective-permute-start.16 = (bf16[1,20,10,128]{3,1,2,0:T(8,128)(2,1)S(1)}, bf16[1,20,10,128]{3,1,2,0:T(8,128)(2,1)S(1)}, u32[]{:S(2)}, u32[]{:S(2)}) collective-permute-start(bf16[1,20,10,128]{3,1,2,0:T(8,128)(2,1)S(1)} %bitcast.136), channel_id=1, source_target_pairs={{0,13},{1,12},{2,15},{3,14},{4,9},{5,8},{6,11},{7,10},{8,5},{9,4},... | collective-permute-start | bytes 153608 | tf_op jit(solution)/shard_map/ppermute | solution.py:105
  189.8 10.4 %collective-permute-start.17 = (bf16[1,20,10,128]{3,1,2,0:T(8,128)(2,1)S(1)}, bf16[1,20,10,128]{3,1,2,0:T(8,128)(2,1)S(1)}, u32[]{:S(2)}, u32[]{:S(2)}) collective-permute-start(bf16[1,20,10,128]{3,1,2,0:T(8,128)(2,1)S(1)} %bitcast.135), channel_id=1, source_target_pairs={{0,14},{1,15},{2,12},{3,13},{4,10},{5,11},{6,8},{7,9},{8,6},{9,7},... | collective-permute-start | bytes 153608 | tf_op jit(solution)/shard_map/ppermute | solution.py:105
  191.8 11.0 %collective-permute-start.18 = (bf16[1,20,10,128]{3,1,2,0:T(8,128)(2,1)S(1)}, bf16[1,20,10,128]{3,1,2,0:T(8,128)(2,1)S(1)}, u32[]{:S(2)}, u32[]{:S(2)}) collective-permute-start(bf16[1,20,10,128]{3,1,2,0:T(8,128)(2,1)S(1)} %bitcast.134), channel_id=1, source_target_pairs={{0,15},{1,14},{2,13},{3,12},{4,11},{5,10},{6,9},{7,8},{8,7},{9,6},... | collective-permute-start | bytes 153608 | tf_op jit(solution)/shard_map/ppermute | solution.py:105
  208.6 9.2 %copy-start.1 = (bf16[320,5120]{1,0:T(8,128)(2,1)S(1)}, bf16[320,5120]{1,0:T(8,128)(2,1)}, u32[]{:S(2)}) copy-start(bf16[320,5120]{1,0:T(8,128)(2,1)} %param.11) | copy-start | bytes 9830404
